TPU v7x, 32 devices: a whole 2x2x4 slice. The times are simulated.
32 devices in a mesh: ctx: 8 (over y, x, core), head: 4 (over z).
Axes of the slice: x: 2, y: 2, z: 4, core: 2. Of those that a mesh axis runs over, the one named last changes fastest.
Arguments:
- xs: bfloat16 [4096, 5120], P('ctx', 'head'), may hold values from -6 to 6
- bmat: bfloat16 [4096, 128], P('ctx'), may hold values from -0.5 to 0.5
- cmat: bfloat16 [4096, 128], P('ctx'), may hold values from -6 to 6
- logdecay: float32 [80, 4096], P('head', 'ctx'), may hold values from -1 to 0, as said below
- starts: int32 [4096], P('ctx'), may hold values 0 or 1
- output_cotangent: bfloat16 [4096, 5120], P('ctx', 'head'), may hold values from -6 to 6
Outputs:
- input_gradient: bfloat16 [4096, 5120], P('ctx', 'head')
- grad_b: float32 [4096, 128], P(('ctx', 'head'))
- grad_c: float32 [4096, 128], P(('ctx', 'head'))
Inputs may be any that keep to these rules, and one draw needn't show every extreme that they name: `logdecay`: every entry is negative.
All inputs are finite; a program needn't handle non-finite values. No bound on the sum of `starts` on one device may be relied on, other than what follows from the above.
Results may differ from a plain program's by a relative error of at most 0.001.
Values sent between devices are 32-bit elements; how exact they have to be, the bound alone decides.
A program may use at most 256 MiB of HBM per device.

v0:
```python
import jax
import jax.numpy as jnp
from jax import lax
from jax.sharding import PartitionSpec as P

P_SIZE = 64
N = 128
Q = 256


HIGH = lax.Precision.HIGHEST


def entering_2(value, axis, combine, identity, reverse):
    devices, mine = (lax.axis_size(axis), lax.axis_index(axis))
    everything = jax.tree.map(lambda part: lax.all_gather(part, axis), value)
    start = jax.tree.map(
        lambda part, zero: jnp.broadcast_to(jnp.asarray(zero, part.dtype), part.shape),
        value,
        identity,
    )

    def turn(k, before):
        at = devices - 1 - k if reverse else k
        reached = at > mine if reverse else at < mine
        new = combine(before, jax.tree.map(lambda part: part[at], everything))
        return jax.tree.map(lambda a, b: jnp.where(reached, a, b), new, before)

    return lax.fori_loop(0, devices, turn, start)


def block_edges(decay_rows, flag_row):
    width = flag_row.shape[0]
    upper = (
        lax.broadcasted_iota(jnp.int32, (width, width), 0)
        <= lax.broadcasted_iota(jnp.int32, (width, width), 1)
    ).astype(jnp.float32)
    running = jnp.dot(decay_rows, upper, precision=HIGH)
    segment = jnp.cumsum(flag_row)
    enter = jnp.where(segment[None, :] == 0, jnp.exp(running), 0.0)
    tail = jnp.where(segment[None, :] == segment[-1], jnp.exp(running[:, -1:] - running), 0.0)
    passing = jnp.where(segment[-1] == 0, jnp.exp(running[:, -1]), 0.0)
    return (running, segment, enter, tail, passing)


def block_within(running, segment):
    width = segment.shape[0]
    rows = lax.broadcasted_iota(jnp.int32, (width, width), 0)
    cols = lax.broadcasted_iota(jnp.int32, (width, width), 1)
    keep = (rows >= cols) & (segment[:, None] == segment[None, :])
    gap = running[:, :, None] - running[:, None, :]
    return jnp.where(keep[None], jnp.exp(jnp.minimum(gap, 0.0)), 0.0)


def combine(earlier, later):
    return (earlier[0] * later[0], later[1] + later[0][:, None, None] * earlier[1])


def chain_step(carry, item):
    factor, state = carry
    through, fresh = item
    return ((factor * through, through[:, None, None] * state + fresh), (factor, state))


def intra_block(item):
    running, segment, scaled, upstream32, keys32, reads32 = item
    within = block_within(running, segment)
    scores = jnp.dot(reads32, keys32.T, precision=HIGH)
    weighted = within * scores[None]
    back_x = jnp.einsum("hts,thp->shp", weighted, upstream32, precision=HIGH)
    pairing = jnp.einsum("thp,shp->hts", upstream32, scaled, precision=HIGH)
    mixed = jnp.sum(within * pairing, axis=0)
    grad_read = jnp.dot(mixed, keys32, precision=HIGH)
    grad_key = jnp.dot(mixed.T, reads32, precision=HIGH)
    return (back_x, grad_key, grad_read)


def device_carries(device_forward, device_backward, start):
    incoming = entering_2(device_forward, "ctx", combine, start, False)[1]
    outgoing = entering_2(device_backward, "ctx", combine, start, True)[1]
    return (incoming, outgoing)


def shards(xs, bmat, cmat, logdecay, starts, output_cotangent):
    token_stream = xs.shape[0]
    heads = logdecay.shape[0]
    count = token_stream // Q
    upstream32 = output_cotangent.reshape(count, Q, heads, P_SIZE).astype(jnp.float32)
    keys32 = bmat.reshape(count, Q, N).astype(jnp.float32)
    reads32 = cmat.reshape(count, Q, N).astype(jnp.float32)
    decays = logdecay.reshape(heads, count, Q).transpose(1, 0, 2)
    flags = starts.reshape(count, Q)
    running, segment, enter, tail, passing = jax.vmap(block_edges)(decays, flags)
    gain = jnp.swapaxes(jnp.sqrt(-jnp.expm1(2.0 * decays)), 1, 2)[..., None]
    tail_rows = jnp.swapaxes(tail, 1, 2)[..., None]
    enter_rows = jnp.swapaxes(enter, 1, 2)[..., None]
    scaled = xs.reshape(count, Q, heads, P_SIZE).astype(jnp.float32) * gain
    tailed = scaled * tail_rows
    entered = upstream32 * enter_rows
    local_state = jnp.einsum("cshp,csn->chpn", tailed, keys32, precision=HIGH)
    local_adjoint = jnp.einsum("cthp,ctn->chpn", entered, reads32, precision=HIGH)
    start = (jnp.ones((heads,), jnp.float32), jnp.zeros((heads, P_SIZE, N), jnp.float32))
    device_forward, (before_factor, before_state) = lax.scan(
        chain_step, start, (passing, local_state)
    )
    device_backward, (after_factor, later_state_adjoint) = lax.scan(
        chain_step, start, (passing, local_adjoint), reverse=True
    )
    forward_part = (device_forward[0], device_forward[1])
    backward_part = (device_backward[0], device_backward[1])
    leading_portion = (start[0], start[1])
    incoming_group, exiting_state_group = device_carries(
        forward_part, backward_part, leading_portion
    )
    pieces = (running, segment, scaled, upstream32, keys32, reads32)
    group_x, group_key, group_read = lax.map(intra_block, pieces)
    entering = before_state + before_factor[:, :, None, None] * incoming_group[None]
    leaving = later_state_adjoint + after_factor[:, :, None, None] * exiting_state_group[None]
    state_x = jnp.einsum("chpn,csn->cshp", leaving, keys32, precision=HIGH) * tail_rows
    state_key = jnp.einsum("chpn,cshp->csn", leaving, tailed, precision=HIGH)
    state_read = jnp.einsum("chpn,cthp->ctn", entering, entered, precision=HIGH)
    input_gradient = (
        ((group_x + state_x) * gain).astype(jnp.bfloat16).reshape(token_stream, heads * P_SIZE)
    )
    key_rows = (group_key + state_key).reshape(token_stream, N)
    read_rows = (group_read + state_read).reshape(token_stream, N)
    grad_b, grad_c = (
        lax.psum_scatter(key_rows, "head", scatter_dimension=0, tiled=True),
        lax.psum_scatter(read_rows, "head", scatter_dimension=0, tiled=True),
    )
    return (input_gradient, grad_b, grad_c)


def solution(mesh):
    in_specs = (
        P("ctx", "head"),
        P("ctx", None),
        P("ctx", None),
        P("head", "ctx"),
        P("ctx"),
        P("ctx", "head"),
    )
    out_specs = (P("ctx", "head"), P(("ctx", "head"), None), P(("ctx", "head"), None))
    return jax.shard_map(shards, mesh=mesh, in_specs=in_specs, out_specs=out_specs, check_vma=False)
```

profile of v0, /device:TPU:0, one launch (start us, length us, event | category | flops | bytes accessed | tf_op | source)
XLA Modules:
  0.0 162.4 jit_solution(16535837869734895685)
XLA Ops:
  10.5 2.8 %copy.24 = f32[512,1280]{0,1:T(8,128)} copy(bf16[512,1280]{1,0:T(8,128)(2,1)} %param.16) | data formatting | bytes 3932160 | tf_op jit(solution)/shard_map/convert_element_type | solution.py:97
  13.4 3.3 %reshape.149 = f32[2,256,20,64]{1,0,3,2:T(2,128)S(1)} reshape(f32[512,1280]{0,1:T(8,128)} %copy.24) | data formatting | bytes 5242880 | tf_op jit(solution)/shard_map/convert_element_type | solution.py:97
  21.2 2.8 %copy.22 = f32[512,1280]{0,1:T(8,128)} copy(bf16[512,1280]{1,0:T(8,128)(2,1)} %param.21) | data formatting | bytes 3932160 | tf_op jit(solution)/shard_map/convert_element_type | solution.py:88
  23.9 3.3 %reshape.148 = f32[2,256,20,64]{1,0,3,2:T(2,128)S(1)} reshape(f32[512,1280]{0,1:T(8,128)} %copy.22) | data formatting | bytes 5242880 | tf_op jit(solution)/shard_map/convert_element_type | solution.py:88
  28.4 2.4 %fusion.45 = f32[2,20,64,128]{3,2,1,0:T(8,128)} fusion(bf16[2,256,128,1]{2,1,3,0:T(8,128)(2,1)S(1)} %bitcast.191, f32[2,256,20,64]{1,0,3,2:T(2,128)S(1)} %broadcast_multiply_fusion), kind=kOutput, calls=%fused_computation.64 | convolution fusion | flops 1006632960 | bytes 4063232 | tf_op jit(solution)/shard_map/cthp,ctn->chpn/dot_general | solution.py:101
  32.0 4.3 %while.83 = (s32[]{:T(128)}, f32[20]{0:T(128)S(1)}, f32[20,64,128]{2,1,0:T(8,128)S(1)}, f32[2,20]{1,0:T(2,128)S(1)}, f32[2,20,64,128]{3,2,1,0:T(8,128)}, /*index...) while((s32[]{:T(128)}, f32[20]{0:T(128)S(1)}, ...), condition=%wide.region_6.7_spmd.clone, body=%wide.region_5.6_spmd.clone.sunk | while | flops 655404 | bytes 3277573 | solution.py:106
  39.0 16.2 %all-reduce.2 = (f32[160]{0:T(256)}, f32[160]{0:T(256)S(1)}) all-reduce(f32[160]{0:T(256)S(1)} %dynamic-update-slice, f32[160]{0:T(256)S(1)} %dynamic-update-slice.1), channel_id=3, replica_groups=mesh['ctx'=8,'head'=4] {'ctx'}, use_global_device_ids=true, to_apply=%add | all-reduce | flops 320 | bytes 2560
  58.5 31.6 %while.82 = (s32[]{:T(128)}, f32[2,256,20,64]{1,3,2,0:T(8,128)}, f32[2,256,128]{2,1,0:T(8,128)}, f32[2,256,128]{2,1,0:T(8,128)}, f32[2,256,20,64]{1,0,3,2:T(2,12...) while((s32[]{:T(128)}, f32[2,256,20,64]{1,3,2,0:T(8,128)}, ...), condition=%wide.region_4.5_spmd, body=%wide.region_2.4_spmd.sunk | while | flops 2327183360 | bytes 42973452 | solution.py:116
  61.5 4.5 %fusion.118 = f32[2,256,20,64]{1,3,2,0:T(8,128)S(1)} fusion(f32[2,256,20,64]{1,3,2,0:T(8,128)S(1)} %copy-done.8, s32[]{:T(128)} %get-tuple-element.902, f32[256,256]{1,0:T(8,128)S(1)} %fusion.116, f32[20,256]{1,0:T(8,128)S(1)} %dynamic-slice_bitcast_fusion.6, pred[256,256]{1,0:T(8,128)(4,1)S(1)} %fusion.117, ...), kind=kOutput, calls=%fused_computation.10.clone.1 | convolution fusion | flops 1011875840 | bytes 2998276 | tf_op jit(solution)/shard_map/while/body/eval_jaxpr/hts,thp->shp/dot_general | solution.py:70
  66.0 6.0 %multiply_reduce_fusion.2 = f32[256,256]{1,0:T(8,128)S(1)} fusion(f32[20,256]{1,0:T(8,128)S(1)} %dynamic-slice_bitcast_fusion.6, pred[256,256]{1,0:T(8,128)(4,1)S(1)} %fusion.117, f32[2,256,20,64]{1,3,2,0:T(8,128)S(1)} %copy-done.4, s32[]{:T(128)} %get-tuple-element.902, f32[1,256,20,64]{1,0,3,2:T(1,128)S(1)} %constant_dynamic-slice_fusion.7), kind=kOutput, calls=%fused_computation.clone.1 | convolution fusion | flops 1013121024 | bytes 2998276 | tf_op jit(solution)/shard_map/while/body/eval_jaxpr/thp,shp->hts/dot_general | solution.py:71
  77.3 4.5 %fusion.118 = f32[2,256,20,64]{1,3,2,0:T(8,128)S(1)} fusion(f32[2,256,20,64]{1,3,2,0:T(8,128)S(1)} %copy-done.8, s32[]{:T(128)} %get-tuple-element.902, f32[256,256]{1,0:T(8,128)S(1)} %fusion.116, f32[20,256]{1,0:T(8,128)S(1)} %dynamic-slice_bitcast_fusion.6, pred[256,256]{1,0:T(8,128)(4,1)S(1)} %fusion.117, ...), kind=kOutput, calls=%fused_computation.10.clone.1 | convolution fusion | flops 1011875840 | bytes 2998276 | tf_op jit(solution)/shard_map/while/body/eval_jaxpr/hts,thp->shp/dot_general | solution.py:70
  81.8 6.0 %multiply_reduce_fusion.2 = f32[256,256]{1,0:T(8,128)S(1)} fusion(f32[20,256]{1,0:T(8,128)S(1)} %dynamic-slice_bitcast_fusion.6, pred[256,256]{1,0:T(8,128)(4,1)S(1)} %fusion.117, f32[2,256,20,64]{1,3,2,0:T(8,128)S(1)} %copy-done.4, s32[]{:T(128)} %get-tuple-element.902, f32[1,256,20,64]{1,0,3,2:T(1,128)S(1)} %constant_dynamic-slice_fusion.7), kind=kOutput, calls=%fused_computation.clone.1 | convolution fusion | flops 1013121024 | bytes 2998276 | tf_op jit(solution)/shard_map/while/body/eval_jaxpr/thp,shp->hts/dot_general | solution.py:71
  90.1 18.0 %while.86 = (s32[]{:T(128)}, f32[20,64,128]{2,1,0:T(8,128)}, s32[]{:T(128)}, f32[8,20,64,128]{3,2,1,0:T(8,128)}, f32[8,20]{1,0:T(8,128)S(1)}, /*index=5*/s32[]{:T(128)}, s32[]{:T(128)}) while((s32[]{:T(128)}, f32[20,64,128]{2,1,0:T(8,128)}, s32[]{:T(128)}, f32[8,20,64,128]{3,2,1,0:T(8,128)}, f32[8,20]{1,0:T(8,128)S(1)}, ...), condition=%wide.region_13.14_spmd.clone, body=%wide.region_12.13_spmd.clone.sunk | while | flops 655364 | bytes 1966425 | solution.py:29
  92.2 2.3 %fusion.124 = f32[20,64,128]{2,1,0:T(8,128)} fusion(f32[20,64,128]{2,1,0:T(8,128)} %get-tuple-element.1013, f32[8,20,64,128]{3,2,1,0:T(8,128)} %get-tuple-element.1022, s32[]{:T(128)} %get-tuple-element.1012, f32[20]{0:T(128)S(1)} %dynamic-slice_bitcast_fusion.8, pred[]{:T(512)S(6)} %compare.15, pred[]{:T(512)S(6)} %lt.63), kind=kLoop, calls=%fused_computation.55.clone.1 | loop fusion | flops 655360 | bytes 1966166 | tf_op jit(solution)/shard_map/while/body/eval_jaxpr/jit(_where)/select_n | solution.py:27
  94.5 2.3 %fusion.124 = f32[20,64,128]{2,1,0:T(8,128)} fusion(f32[20,64,128]{2,1,0:T(8,128)} %get-tuple-element.1013, f32[8,20,64,128]{3,2,1,0:T(8,128)} %get-tuple-element.1022, s32[]{:T(128)} %get-tuple-element.1012, f32[20]{0:T(128)S(1)} %dynamic-slice_bitcast_fusion.8, pred[]{:T(512)S(6)} %compare.15, pred[]{:T(512)S(6)} %lt.63), kind=kLoop, calls=%fused_computation.55.clone.1 | loop fusion | flops 655360 | bytes 1966166 | tf_op jit(solution)/shard_map/while/body/eval_jaxpr/jit(_where)/select_n | solution.py:27
  96.8 2.3 %fusion.124 = f32[20,64,128]{2,1,0:T(8,128)} fusion(f32[20,64,128]{2,1,0:T(8,128)} %get-tuple-element.1013, f32[8,20,64,128]{3,2,1,0:T(8,128)} %get-tuple-element.1022, s32[]{:T(128)} %get-tuple-element.1012, f32[20]{0:T(128)S(1)} %dynamic-slice_bitcast_fusion.8, pred[]{:T(512)S(6)} %compare.15, pred[]{:T(512)S(6)} %lt.63), kind=kLoop, calls=%fused_computation.55.clone.1 | loop fusion | flops 655360 | bytes 1966166 | tf_op jit(solution)/shard_map/while/body/eval_jaxpr/jit(_where)/select_n | solution.py:27
  99.0 2.3 %fusion.124 = f32[20,64,128]{2,1,0:T(8,128)} fusion(f32[20,64,128]{2,1,0:T(8,128)} %get-tuple-element.1013, f32[8,20,64,128]{3,2,1,0:T(8,128)} %get-tuple-element.1022, s32[]{:T(128)} %get-tuple-element.1012, f32[20]{0:T(128)S(1)} %dynamic-slice_bitcast_fusion.8, pred[]{:T(512)S(6)} %compare.15, pred[]{:T(512)S(6)} %lt.63), kind=kLoop, calls=%fused_computation.55.clone.1 | loop fusion | flops 655360 | bytes 1966166 | tf_op jit(solution)/shard_map/while/body/eval_jaxpr/jit(_where)/select_n | solution.py:27
  101.3 2.3 %fusion.124 = f32[20,64,128]{2,1,0:T(8,128)} fusion(f32[20,64,128]{2,1,0:T(8,128)} %get-tuple-element.1013, f32[8,20,64,128]{3,2,1,0:T(8,128)} %get-tuple-element.1022, s32[]{:T(128)} %get-tuple-element.1012, f32[20]{0:T(128)S(1)} %dynamic-slice_bitcast_fusion.8, pred[]{:T(512)S(6)} %compare.15, pred[]{:T(512)S(6)} %lt.63), kind=kLoop, calls=%fused_computation.55.clone.1 | loop fusion | flops 655360 | bytes 1966166 | tf_op jit(solution)/shard_map/while/body/eval_jaxpr/jit(_where)/select_n | solution.py:27
  105.9 2.3 %fusion.124 = f32[20,64,128]{2,1,0:T(8,128)} fusion(f32[20,64,128]{2,1,0:T(8,128)} %get-tuple-element.1013, f32[8,20,64,128]{3,2,1,0:T(8,128)} %get-tuple-element.1022, s32[]{:T(128)} %get-tuple-element.1012, f32[20]{0:T(128)S(1)} %dynamic-slice_bitcast_fusion.8, pred[]{:T(512)S(6)} %compare.15, pred[]{:T(512)S(6)} %lt.63), kind=kLoop, calls=%fused_computation.55.clone.1 | loop fusion | flops 655360 | bytes 1966166 | tf_op jit(solution)/shard_map/while/body/eval_jaxpr/jit(_where)/select_n | solution.py:27
  108.2 7.5 %fusion.66 = f32[2,256,128]{2,1,0:T(8,128)} fusion(f32[2,256,128]{2,1,0:T(8,128)} %get-tuple-element.474, f32[2,20,64,128]{3,2,1,0:T(8,128)} %copy-done.7, f32[2,256,20,64]{1,0,3,2:T(2,128)} %copy-done.2, f32[20,64,128]{2,1,0:T(8,128)} %get-tuple-element.479, f32[2,20]{1,0:T(2,128)S(1)} %get-tuple-element.476), kind=kOutput, calls=%fused_computation.79 | convolution fusion | flops 1007353856 | bytes 5111968 | tf_op jit(solution)/shard_map/chpn,cthp->ctn/dot_general | solution.py:121
  115.8 10.3 %while.84 = (s32[]{:T(128)}, f32[20,64,128]{2,1,0:T(8,128)S(1)}, s32[]{:T(128)}, f32[8,20,64,128]{3,2,1,0:T(8,128)}, f32[8,20]{1,0:T(8,128)S(1)}, /*index=5*/s32[]{:T(128)}, s32[]{:T(128)}, s32[]{:T(128)}, s32[]{:T(128)}) while((s32[]{:T(128)}, f32[20,64,128]{2,1,0:T(8,128)S(1)}, s32[]{:T(128)}, f32[8,20,64,128]{3,2,1,0:T(8,128)}, ...), condition=%wide.region_8.9_spmd.clone, body=%wide.region_7.8_spmd.clone.sunk | while | flops 655368 | bytes 1966487 | solution.py:29
  126.1 6.4 %fusion.63 = f32[2,256,128]{2,1,0:T(8,128)} fusion(f32[2,256,128]{2,1,0:T(8,128)} %get-tuple-element.473, f32[2,256,20,64]{1,3,2,0:T(8,128)S(1)} %copy-done.5, f32[2,256,20]{1,2,0:T(8,128)S(1)} %copy-done.13, f32[2,20,64,128]{3,2,1,0:T(8,128)} %get-tuple-element.468, f32[20,64,128]{2,1,0:T(8,128)S(1)} %get-tuple-element.472, f32[2,20]{1,0:T(2,128)S(1)} %copy-done.20), kind=kOutput, calls=%fused_computation.78 | convolution fusion | flops 1008009216 | bytes 5152928 | tf_op jit(solution)/shard_map/chpn,cshp->csn/dot_general | solution.py:120
  132.6 3.5 %fusion.42 = bf16[2,256,20,64]{1,3,2,0:T(8,128)(2,1)S(1)} fusion(f32[2,256,20,64]{1,3,2,0:T(8,128)} %get-tuple-element.467, bf16[2,256,128,1]{2,1,3,0:T(8,128)(2,1)S(1)} %bitcast.185, f32[2,256,20]{1,2,0:T(8,128)S(1)} %copy-done.13, f32[2,256,20]{1,2,0:T(8,128)S(1)} %copy-done.18, f32[2,20,64,128]{3,2,1,0:T(8,128)} %get-tuple-element.468, ...), kind=kOutput, calls=%fused_computation.60 | convolution fusion | flops 1009909760 | bytes 6111392 | tf_op jit(solution)/shard_map/chpn,csn->cshp/dot_general | solution.py:119
  139.2 16.6 %reduce-scatter.3.cloned.1.call-done = f32[128,128]{1,0:T(8,128)} async-done(((f32[512,128]{1,0:T(8,128)}), f32[128,128]{1,0:T(8,128)}) %reduce-scatter.3.cloned.1.call-update) | async-done | bytes 65552 | tf_op jit(solution)/shard_map/reduce_scatter | solution.py:128
  (165 shorter events, 48.2 us)
Async XLA Ops:
  7.2 83.0 %all-gather.9.cloned.1.call-start = ((), (), s32[]{:S(2)}) async-start(), calls=%async_computation.5 | async-start | bytes 5898240 | tf_op jit(solution)/shard_map/all_gather | solution.py:16
  8.3 8.5 %copy-start.14 = (f32[256,2,20]{0,2,1:T(8,128)}, f32[256,2,20]{0,2,1:T(8,128)S(1)}, u32[]{:S(2)}) copy-start(f32[256,2,20]{0,2,1:T(8,128)S(1)} %fusion.78) | copy-start | bytes 122884
  8.3 8.5 %copy-start.17 = (f32[2,256,20]{1,2,0:T(8,128)}, f32[2,256,20]{1,2,0:T(8,128)S(1)}, u32[]{:S(2)}) copy-start(f32[2,256,20]{1,2,0:T(8,128)S(1)} %fusion.83) | copy-start | bytes 122884
  20.8 95.0 %all-gather.7.cloned.1.call-start = ((), (), s32[]{:S(2)}) async-start(), calls=%async_computation.4 | async-start | bytes 5898240 | tf_op jit(solution)/shard_map/all_gather | solution.py:16
  28.4 3.6 %copy-start.2 = (f32[2,256,20,64]{1,0,3,2:T(2,128)}, f32[2,256,20,64]{1,0,3,2:T(2,128)S(1)}, u32[]{:S(2)}) copy-start(f32[2,256,20,64]{1,0,3,2:T(2,128)S(1)} %broadcast_multiply_fusion) | copy-start | bytes 7864324
  32.0 5.3 %copy-start.21 = (u32[32]{0:T(128)S(1)}, u32[32]{0:T(128)}, u32[]{:S(2)}) copy-start(u32[32]{0:T(128)} %constant.162) | copy-start | bytes 388
  36.3 18.9 %copy-start.19 = (f32[2,20]{1,0:T(2,128)}, f32[2,20]{1,0:T(2,128)S(1)}, u32[]{:S(2)}) copy-start(f32[2,20]{1,0:T(2,128)S(1)} %get-tuple-element.469) | copy-start | bytes 484
  37.2 102.1 %reduce-scatter.5.cloned.1.call-start = ((), (), s32[]{:S(2)}) async-start(), calls=%async_computation.3 | async-start | bytes 327680 | tf_op jit(solution)/shard_map/reduce_scatter | solution.py:129
  58.5 3.0 %copy-start.15 = (f32[2,20,256]{2,1,0:T(8,128)S(1)}, f32[2,20,256]{2,1,0:T(8,128)}, u32[]{:S(2)}) copy-start(f32[2,20,256]{2,1,0:T(8,128)} %get-tuple-element.919) | copy-start | bytes 122884 | tf_op jit(solution)/shard_map/while
  58.5 3.0 %copy-start.8 = (f32[2,256,20,64]{1,3,2,0:T(8,128)S(1)}, f32[2,256,20,64]{1,3,2,0:T(8,128)}, u32[]{:S(2)}) copy-start(f32[2,256,20,64]{1,3,2,0:T(8,128)} %get-tuple-element.903) | copy-start | bytes 7864324 | tf_op jit(solution)/shard_map/while
  61.5 4.5 %copy-start.4 = (f32[2,256,20,64]{1,3,2,0:T(8,128)S(1)}, f32[2,256,20,64]{1,3,2,0:T(8,128)}, u32[]{:S(2)}) copy-start(f32[2,256,20,64]{1,3,2,0:T(8,128)} %get-tuple-element.922) | copy-start | bytes 7864324 | tf_op jit(solution)/shard_map/while
  66.0 6.0 %copy-start.9 = (f32[2,256,20,64]{1,3,2,0:T(8,128)}, f32[2,256,20,64]{1,3,2,0:T(8,128)S(1)}, u32[]{:S(2)}) copy-start(f32[2,256,20,64]{1,3,2,0:T(8,128)S(1)} %fusion.118) | copy-start | bytes 7864324 | tf_op jit(solution)/shard_map/while
  66.0 7.3 %copy-start.6 = (f32[2,256,128]{2,1,0:T(8,128)S(1)}, f32[2,256,128]{2,1,0:T(8,128)}, u32[]{:S(2)}) copy-start(f32[2,256,128]{2,1,0:T(8,128)} %get-tuple-element.921) | copy-start | bytes 786436 | tf_op jit(solution)/shard_map/while
  74.3 3.0 %copy-start.15 = (f32[2,20,256]{2,1,0:T(8,128)S(1)}, f32[2,20,256]{2,1,0:T(8,128)}, u32[]{:S(2)}) copy-start(f32[2,20,256]{2,1,0:T(8,128)} %get-tuple-element.919) | copy-start | bytes 122884 | tf_op jit(solution)/shard_map/while
  74.3 3.0 %copy-start.8 = (f32[2,256,20,64]{1,3,2,0:T(8,128)S(1)}, f32[2,256,20,64]{1,3,2,0:T(8,128)}, u32[]{:S(2)}) copy-start(f32[2,256,20,64]{1,3,2,0:T(8,128)} %get-tuple-element.903) | copy-start | bytes 7864324 | tf_op jit(solution)/shard_map/while
  77.3 4.5 %copy-start.4 = (f32[2,256,20,64]{1,3,2,0:T(8,128)S(1)}, f32[2,256,20,64]{1,3,2,0:T(8,128)}, u32[]{:S(2)}) copy-start(f32[2,256,20,64]{1,3,2,0:T(8,128)} %get-tuple-element.922) | copy-start | bytes 7864324 | tf_op jit(solution)/shard_map/while
  81.8 6.0 %copy-start.9 = (f32[2,256,20,64]{1,3,2,0:T(8,128)}, f32[2,256,20,64]{1,3,2,0:T(8,128)S(1)}, u32[]{:S(2)}) copy-start(f32[2,256,20,64]{1,3,2,0:T(8,128)S(1)} %fusion.118) | copy-start | bytes 7864324 | tf_op jit(solution)/shard_map/while
  81.8 7.3 %copy-start.6 = (f32[2,256,128]{2,1,0:T(8,128)S(1)}, f32[2,256,128]{2,1,0:T(8,128)}, u32[]{:S(2)}) copy-start(f32[2,256,128]{2,1,0:T(8,128)} %get-tuple-element.921) | copy-start | bytes 786436 | tf_op jit(solution)/shard_map/while
  108.2 17.9 %copy-start.5 = (f32[2,256,20,64]{1,3,2,0:T(8,128)S(1)}, f32[2,256,20,64]{1,3,2,0:T(8,128)}, u32[]{:S(2)}) copy-start(f32[2,256,20,64]{1,3,2,0:T(8,128)} %get-tuple-element.1034) | copy-start | bytes 7864324
  115.7 40.1 %reduce-scatter.3.cloned.1.call-start = ((), (), s32[]{:S(2)}) async-start(), calls=%async_computation.2 | async-start | bytes 327680 | tf_op jit(solution)/shard_map/reduce_scatter | solution.py:128
  115.8 10.3 %copy-start.13 = (f32[2,256,20]{1,2,0:T(8,128)S(1)}, f32[2,256,20]{1,2,0:T(8,128)}, u32[]{:S(2)}) copy-start(f32[2,256,20]{1,2,0:T(8,128)} %copy-done.12) | copy-start | bytes 122884
  115.8 10.3 %copy-start.20 = (f32[2,20]{1,0:T(2,128)S(1)}, f32[2,20]{1,0:T(2,128)}, u32[]{:S(2)}) copy-start(f32[2,20]{1,0:T(2,128)} %copy-done.19) | copy-start | bytes 484
  126.1 6.5 %copy-start.11 = (bf16[512,128]{1,0:T(8,128)(2,1)S(1)}, bf16[512,128]{1,0:T(8,128)(2,1)}, u32[]{:S(2)}) copy-start(bf16[512,128]{1,0:T(8,128)(2,1)} %param.17) | copy-start | bytes 393220
  126.1 6.5 %copy-start.18 = (f32[2,256,20]{1,2,0:T(8,128)S(1)}, f32[2,256,20]{1,2,0:T(8,128)}, u32[]{:S(2)}) copy-start(f32[2,256,20]{1,2,0:T(8,128)} %copy-done.17) | copy-start | bytes 122884
  (7 other events, 7.7 us)
Sparse Core Ops, SparseCore 0:
  20.9 43.9 all-gather.8
  66.7 41.0 all-gather.6
  115.8 19.2 reduce-scatter.4
  137.9 17.8 reduce-scatter.2
where the time goes:
time: 164 us; the launch traced here: 162 us
  matrix products  49.8 us (30%)
  other arithmetic  38.6 us (24%)
  local copies, waits for them, and re-layouts  25.6 us (16%)
  waiting for transfers between devices  16.7 us (10%)
  blocking collectives  16.2 us (10%)
  between operations  14.8 us (9%)
    select_n x16, other arithmetic, turn(): return jax.tree.map(lambda a, b: jnp.where(reached, a, b), new, before)  27.9 us
    reduce_scatter x1, waiting for transfers between devices, shards(): lax.psum_scatter(key_rows, 'head', scatter_dimension=0, tiled=True)  16.6 us
    unnamed x1, blocking collectives  16.2 us
    dot_general x2, matrix products, intra_block(): pairing = jnp.einsum('thp,shp->hts', upstream32, scaled, precision=HIGH)  11.9 us
    dot_general x2, matrix products, intra_block(): back_x = jnp.einsum('hts,thp->shp', weighted, upstream32, precision=HIGH)  8.96 us
    dot_general x1, matrix products, shards(): state_read = jnp.einsum('chpn,cthp->ctn', entering, entered, precision=HIGH)  7.5 us
    dot_general x1, matrix products, shards(): state_key = jnp.einsum('chpn,cshp->csn', leaving, tailed, precision=HIGH)  6.45 us
    convert_element_type x2, local copies, waits for them, and re-layouts, shards(): scaled = xs.reshape(count, Q, heads, P_SIZE).astype(jnp.float32) * gain  6.11 us
  transfers between devices with their start and end apart: 4, of which 1 were waited for; matrix products, arithmetic and copies ran while one was open for 61% of the time, Pallas kernels for 0%

commit v1 on v0

v1 whole, which is shorter than its diff:
```python
import functools

import jax
import jax.numpy as jnp
from jax import lax
from jax.experimental import pallas as pl
from jax.experimental.pallas import tpu as pltpu
from jax.sharding import PartitionSpec as P

P_SIZE = 64
N = 128
Q = 256
LANES = 128
LOG2E = 1.4426950408889634
MESH = pl.DeviceIdType.MESH
F32 = jnp.float32
BF16 = jnp.bfloat16


def nn(a, b):
    return lax.dot_general(a, b, (((1,), (0,)), ((), ())), preferred_element_type=F32)


def nt(a, b):
    return lax.dot_general(a, b, (((1,), (1,)), ((), ())), preferred_element_type=F32)


def split2(value):
    high = value.astype(BF16)
    return high, (value - high.astype(F32)).astype(BF16)


def split3(value):
    high, rest = value.astype(BF16), None
    rest = value - high.astype(F32)
    middle = rest.astype(BF16)
    return high, middle, (rest - middle.astype(F32)).astype(BF16)


def minus_expm1(x):
    series = jnp.ones_like(x)
    for term in range(11, 1, -1):
        series = 1.0 + series * x * (1.0 / term)
    return jnp.where(x > -0.5, -x * series, 1.0 - jnp.exp(x))


def kernel(
    ctx, hd, heads, count,
    xs, bm, cm, ld, st, dy,
    gx_out, gb_out, gc_out,
    ldp, colterm, runrow, factor, expand, passing, bias, scores, mixed,
    keys_t, reads_t, tail_x, t_hi, t_lo, e_hi, e_lo, group, local_s, local_a,
    agg, got0, chip, got, inout, other, final, part, rs_got,
    send_sem, recv_sem, rs_send, rs_recv,
):
    width = heads * P_SIZE
    tiles = width // LANES
    half = tiles // 2
    bits = ctx.bit_length() - 1
    me, row = lax.axis_index("ctx"), lax.axis_index("head")
    bit = [(me // (1 << d)) % 2 for d in range(bits)]
    mate = [me + (1 - 2 * bit[d]) * (1 << d) for d in range(bits)]
    core = bit[0]

    barrier = pltpu.get_barrier_semaphore()
    for d in range(bits):
        pl.semaphore_signal(barrier, inc=1, device_id={"ctx": mate[d]}, device_id_type=MESH)
    for step in range(1, hd):
        pl.semaphore_signal(
            barrier, inc=1, device_id={"head": (row + step) % hd}, device_id_type=MESH
        )

    def remote(src, dst, stage, k, d):
        return pltpu.make_async_remote_copy(
            src_ref=src, dst_ref=dst, send_sem=send_sem.at[stage, k],
            recv_sem=recv_sem.at[stage, k], device_id={"ctx": mate[d]}, device_id_type=MESH,
        )

    rows_i = lax.broadcasted_iota(jnp.int32, (Q, Q), 0)
    cols_i = lax.broadcasted_iota(jnp.int32, (Q, Q), 1)
    tri = jnp.where(rows_i >= cols_i, 1.0, 0.0).astype(BF16)
    eye = jnp.where(rows_i == cols_i, 1.0, 0.0).astype(BF16)
    ldp[...] = jnp.zeros_like(ldp)
    ldp[0:heads, :] = ld[...]
    er = lax.broadcasted_iota(jnp.int32, (LANES, width), 0)
    ec = lax.broadcasted_iota(jnp.int32, (LANES, width), 1)
    expand[...] = jnp.where(
        (ec >= er * P_SIZE) & (ec < er * P_SIZE + P_SIZE), 1.0, 0.0
    ).astype(BF16)
    hp = runrow.shape[1]
    for b in range(count):
        blk = slice(b * Q, (b + 1) * Q)
        flags = jnp.broadcast_to(st[0:1, blk].astype(F32), (LANES, Q)).astype(BF16)
        seg_col = nt(tri, flags)
        seg_row = nt(flags[0:16], tri)
        parts = split3(ldp[:, blk])
        run = nt(tri, parts[0]) + (nt(tri, parts[1]) + nt(tri, parts[2]))
        run_r = nt(parts[0][0:hp], tri) + (nt(parts[1][0:hp], tri) + nt(parts[2][0:hp], tri))
        decay = nt(eye, parts[0]) + nt(eye, parts[1]) + nt(eye, parts[2])
        gain2 = minus_expm1(2.0 * decay)
        gain = jnp.sqrt(gain2)
        runrow[b] = run_r * LOG2E
        colterm[b] = run * LOG2E - (0.5 * LOG2E) * jnp.log(gain2)
        last, seg_last = run[Q - 1 : Q], seg_col[Q - 1 : Q]
        tail = jnp.where(seg_col == seg_last, jnp.exp(last - run), 0.0) * gain
        enter = jnp.where(seg_col == 0.0, jnp.exp(run), 0.0)
        through = jnp.broadcast_to(jnp.where(seg_last == 0.0, jnp.exp(last), 0.0), (16, LANES))
        for i, value in enumerate(split3(tail)):
            factor[b, 0, i] = value
        for i, value in enumerate(split3(enter)):
            factor[b, 1, i] = value
        p3 = split3(through)
        passing[b] = (nn(p3[0], expand[...]) + nn(p3[1], expand[...]) + nn(p3[2], expand[...]))[0:8]
        keep = (cols_i >= rows_i) & (
            jnp.broadcast_to(seg_row[0:1], (Q, Q)) == jnp.broadcast_to(seg_col[:, 0:1], (Q, Q))
        )
        bias[b] = jnp.where(keep, 0.0, -1e30)
        keys_t[b] = nt(eye[0:N, 0:N], bm[blk, :]).astype(BF16)
        reads_t[b] = nt(eye[0:N, 0:N], cm[blk, :]).astype(BF16)
        scores[b] = nt(bm[blk, :], cm[blk, :])

    for k in range(tiles):
        col = slice(k * LANES, (k + 1) * LANES)
        ex = expand[:, col]
        for b in range(count):
            blk = slice(b * Q, (b + 1) * Q)
            tx = nn(factor[b, 0, 0], ex) + (nn(factor[b, 0, 1], ex) + nn(factor[b, 0, 2], ex))
            tail_x[blk, col] = tx
            hi, lo = split2(xs[blk, col].astype(F32) * tx)
            t_hi[blk, col] = hi
            t_lo[blk, col] = lo
            local_s[b, k] = nn(keys_t[b], hi) + nn(keys_t[b], lo)
            ent = nn(factor[b, 1, 0], ex) + (nn(factor[b, 1, 1], ex) + nn(factor[b, 1, 2], ex))
            hi, lo = split2(dy[blk, col].astype(F32) * ent)
            e_hi[blk, col] = hi
            e_lo[blk, col] = lo
            local_a[b, k] = nn(reads_t[b], hi) + nn(reads_t[b], lo)
        forward, backward, through = local_s[0, k], local_a[count - 1, k], passing[0, :, col]
        for b in range(1, count):
            forward = local_s[b, k] + passing[b, 0:1, col] * forward
            through = through * passing[b, :, col]
        for b in range(count - 2, -1, -1):
            backward = local_a[b, k] + passing[b, 0:1, col] * backward
        agg[k, 0:N] = forward
        agg[k, N : 2 * N] = backward
        agg[k, 2 * N : 2 * N + 8] = through

    pl.semaphore_wait(barrier, bits + hd - 1)
    stage0 = [
        remote(agg.at[(1 - core) * half + k], got0.at[k], 0, k, 0) for k in range(half)
    ]
    for copy in stage0:
        copy.start()

    F, B, T = slice(0, N), slice(N, 2 * N), slice(2 * N, 2 * N + 8)
    T1 = slice(2 * N, 2 * N + 1)
    copies = {}
    ahead = {}

    def merge(target, mine, theirs, upper):
        def low(s):
            return jnp.where(upper, theirs(s), mine(s))

        def high(s):
            return jnp.where(upper, mine(s), theirs(s))

        target[F] = high(F) + high(T1) * low(F)
        target[B] = low(B) + low(T1) * high(B)
        target[T] = low(T) * high(T)

    def chip_send(d, k):
        if d == bits - 1:
            copy = remote(
                chip.at[d - 1, k, pl.ds(pl.multiple_of(bit[d] * N, N), N)],
                got.at[d - 1, k, pl.ds(0, N)], d, k, d,
            )
        else:
            copy = remote(chip.at[d - 1, k], got.at[d - 1, k], d, k, d)
        copies[d, k] = copy
        copy.start()

    def stage_core(k):
        stage0[k].wait_recv()
        merge(
            chip.at[0, k], lambda s: agg[core * half + k, s], lambda s: got0[k, s], core == 1
        )
        inout[k] = jnp.zeros((2 * N, LANES), F32)
        ahead[k] = (jnp.ones((1, LANES), F32), jnp.ones((1, LANES), F32))
        chip_send(1, k)

    def stage_chip(d, k):
        copies[d, k].wait_recv()
        upper = bit[d] == 1
        from_before, from_after = ahead[k]
        theirs = got.at[d - 1, k]
        last = d == bits - 1
        inout[k, F] = inout[k, F] + jnp.where(upper, from_before, 0.0) * theirs[F]
        inout[k, B] = inout[k, B] + jnp.where(upper, 0.0, from_after) * theirs[F if last else B]
        if not last:
            ahead[k] = (
                jnp.where(upper, from_before * theirs[T1], from_before),
                jnp.where(upper, from_after, from_after * theirs[T1]),
            )
            mine = chip.at[d - 1, k]
            merge(chip.at[d, k], lambda s: mine[s], lambda s: theirs[s], upper)
            chip_send(d + 1, k)
        else:
            own = agg.at[core * half + k]
            odd = core == 1
            enter0, leave1 = inout[k, F], inout[k, B]
            low_f = jnp.where(odd, got0[k, F], own[F])
            low_t = jnp.where(odd, got0[k, T1], own[T1])
            high_b = jnp.where(odd, own[B], got0[k, B])
            high_t = jnp.where(odd, own[T1], got0[k, T1])
            enter1 = low_f + low_t * enter0
            leave0 = high_b + high_t * leave1
            final[core * half + k, F] = jnp.where(odd, enter1, enter0)
            final[core * half + k, B] = jnp.where(odd, leave1, leave0)
            other[k, F] = jnp.where(odd, enter0, enter1)
            other[k, B] = jnp.where(odd, leave0, leave1)
            copy = remote(other.at[k], final.at[core * half + k], bits, k, 0)
            copies[bits, k] = copy
            copy.start()

    mixed[...] = jnp.zeros_like(mixed)
    lane = lax.broadcasted_iota(jnp.int32, (1, LANES), 1)
    head_mask = [
        jnp.where(lane < P_SIZE, 1.0, 0.0).astype(BF16),
        jnp.where(lane < P_SIZE, 0.0, 1.0).astype(BF16),
    ]
    sub = Q // 2

    def intra(k):
        col = slice(k * LANES, (k + 1) * LANES)
        for b in range(count):
            for part_s in range(2):
                t0 = part_s * sub
                s_in = slice(part_s * sub, (part_s + 1) * sub)
                s_at = slice(b * Q + part_s * sub, b * Q + (part_s + 1) * sub)
                t_at = slice(b * Q + t0, (b + 1) * Q)
                x, u = xs[s_at, col], dy[t_at, col]
                total, mix = None, None
                for h in range(2):
                    head = 2 * k + h
                    uh = u * head_mask[h]
                    pairing = nt(x, uh)
                    within = jnp.exp2(
                        (runrow[b, head : head + 1, t0:] - colterm[b, s_in, head : head + 1])
                        + bias[b, s_in, t0:]
                    )
                    hi, lo = split2(within * scores[b, s_in, t0:])
                    product = nn(hi, uh) + nn(lo, uh)
                    total = product if total is None else total + product
                    mix = within * pairing if mix is None else mix + within * pairing
                mixed[b, s_in, t0:] += mix
                group[s_at, col] = total

    todo = {0: [("core", k) for k in range(half)]}
    for k in range(half):
        todo.setdefault(min(2 * k + 2, tiles - 1), []).append(("chip", 1, k))
    for k in range(tiles):
        intra(k)
        for task in todo.get(k, []):
            if task[0] == "core":
                stage_core(task[1])
            else:
                stage_chip(task[1], task[2])
    for b in range(count):
        blk = slice(b * Q, (b + 1) * Q)
        hi, lo = split2(mixed[b])
        part[0, blk] = nn(hi, cm[blk, :]) + nn(lo, cm[blk, :])
        hi, lo = split2(mixed[b].T)
        part[1, blk] = nn(hi, bm[blk, :]) + nn(lo, bm[blk, :])
    for d in range(2, bits):
        for k in range(half):
            stage_chip(d, k)
    for k in range(half):
        copies[bits, k].wait_recv()

    share = count * Q // hd

    def rs_copy(dest):
        return pltpu.make_async_remote_copy(
            src_ref=part.at[:, pl.ds(dest * share, share)], dst_ref=rs_got.at[row],
            send_sem=rs_send.at[dest], recv_sem=rs_recv.at[row],
            device_id={"head": dest}, device_id_type=MESH,
        )

    def state_of(b, k, forward):
        col = slice(k * LANES, (k + 1) * LANES)
        if forward:
            value = final[k, F]
            for at in range(b):
                value = local_s[at, k] + passing[at, 0:1, col] * value
        else:
            value = final[k, B]
            for at in range(count - 1, b, -1):
                value = local_a[at, k] + passing[at, 0:1, col] * value
        return split2(value)

    for b in range(count):
        blk = slice(b * Q, (b + 1) * Q)
        key, read = part[0, blk], part[1, blk]
        for k in range(tiles):
            col = slice(k * LANES, (k + 1) * LANES)
            hi, lo = state_of(b, k, False)
            x_hi = t_hi[blk, col]
            key += nt(x_hi, hi) + (nt(x_hi, lo) + nt(t_lo[blk, col], hi))
            hi, lo = state_of(b, k, True)
            y_hi = e_hi[blk, col]
            read += nt(y_hi, hi) + (nt(y_hi, lo) + nt(e_lo[blk, col], hi))
        part[0, blk] = key
        part[1, blk] = read
        for dest in range(hd):
            if b * Q < (dest + 1) * share <= (b + 1) * Q:
                @pl.when(row != dest)
                def _(dest=dest):
                    rs_copy(dest).start()
    for b in range(count):
        blk = slice(b * Q, (b + 1) * Q)
        for k in range(tiles):
            col = slice(k * LANES, (k + 1) * LANES)
            hi, lo = state_of(b, k, False)
            state_x = nn(bm[blk, :], hi) + nn(bm[blk, :], lo)
            gx_out[blk, col] = (group[blk, col] + state_x * tail_x[blk, col]).astype(BF16)
    mine = pl.ds(pl.multiple_of(row * share, share), share)
    gb_out[...] = part[0, mine]
    gc_out[...] = part[1, mine]
    for source in range(hd):
        @pl.when(row != source)
        def _(source=source):
            pltpu.make_async_remote_copy(
                src_ref=part.at[:, pl.ds(0, share)], dst_ref=rs_got.at[source],
                send_sem=rs_send.at[source], recv_sem=rs_recv.at[source],
                device_id={"head": source}, device_id_type=MESH,
            ).wait_recv()
            gb_out[...] += rs_got[source, 0]
            gc_out[...] += rs_got[source, 1]
    for dest in range(hd):
        @pl.when(row != dest)
        def _(dest=dest):
            rs_copy(dest).wait_send()
    for copy in stage0:
        copy.wait_send()
    for copy in copies.values():
        copy.wait_send()


def shards(ctx, hd, xs, bmat, cmat, logdecay, starts, output_cotangent):
    tokens, width = xs.shape
    heads = logdecay.shape[0]
    count = tokens // Q
    tiles = width // LANES
    half = tiles // 2
    bits = ctx.bit_length() - 1
    head_rows = (heads + 15) // 16 * 16
    share = tokens // hd
    packet = 2 * N + 8
    scratch = [
        pltpu.VMEM((LANES, tokens), F32),
        pltpu.VMEM((count, Q, LANES), F32),
        pltpu.VMEM((count, head_rows, Q), F32),
        pltpu.VMEM((count, 2, 3, Q, LANES), BF16),
        pltpu.VMEM((LANES, width), BF16),
        pltpu.VMEM((count, 8, width), F32),
        pltpu.VMEM((count, Q, Q), F32),
        pltpu.VMEM((count, Q, Q), F32),
        pltpu.VMEM((count, Q, Q), F32),
        pltpu.VMEM((count, N, Q), BF16),
        pltpu.VMEM((count, N, Q), BF16),
        pltpu.VMEM((tokens, width), F32),
        pltpu.VMEM((tokens, width), BF16),
        pltpu.VMEM((tokens, width), BF16),
        pltpu.VMEM((tokens, width), BF16),
        pltpu.VMEM((tokens, width), BF16),
        pltpu.VMEM((tokens, width), F32),
        pltpu.VMEM((count, tiles, N, LANES), F32),
        pltpu.VMEM((count, tiles, N, LANES), F32),
        pltpu.VMEM((tiles, packet, LANES), F32),
        pltpu.VMEM((half, packet, LANES), F32),
        pltpu.VMEM((bits - 1, half, packet, LANES), F32),
        pltpu.VMEM((bits - 1, half, packet, LANES), F32),
        pltpu.VMEM((half, 2 * N, LANES), F32),
        pltpu.VMEM((half, 2 * N, LANES), F32),
        pltpu.VMEM((tiles, 2 * N, LANES), F32),
        pltpu.VMEM((2, tokens, N), F32),
        pltpu.VMEM((hd, 2, share, N), F32),
        pltpu.SemaphoreType.DMA((bits + 1, half)),
        pltpu.SemaphoreType.DMA((bits + 1, half)),
        pltpu.SemaphoreType.DMA((hd,)),
        pltpu.SemaphoreType.DMA((hd,)),
    ]
    vmem = pl.BlockSpec(memory_space=pltpu.VMEM)
    return pl.pallas_call(
        functools.partial(kernel, ctx, hd, heads, count),
        out_shape=(
            jax.ShapeDtypeStruct((tokens, width), BF16),
            jax.ShapeDtypeStruct((share, N), F32),
            jax.ShapeDtypeStruct((share, N), F32),
        ),
        in_specs=[vmem] * 6,
        out_specs=(vmem,) * 3,
        scratch_shapes=scratch,
        compiler_params=pltpu.CompilerParams(
            collective_id=0, has_side_effects=True, vmem_limit_bytes=56 * 1024 * 1024
        ),
    )(xs, bmat, cmat, logdecay, starts.reshape(1, tokens), output_cotangent)


def solution(mesh):
    in_specs = (
        P("ctx", "head"),
        P("ctx", None),
        P("ctx", None),
        P("head", "ctx"),
        P("ctx"),
        P("ctx", "head"),
    )
    out_specs = (P("ctx", "head"), P(("ctx", "head"), None), P(("ctx", "head"), None))
    body = functools.partial(shards, mesh.shape["ctx"], mesh.shape["head"])
    return jax.shard_map(body, mesh=mesh, in_specs=in_specs, out_specs=out_specs, check_vma=False)
```

time: 164 us -> 59.6 us (0.36)
  the two profiles are of different devices: /device:TPU:0 before, /device:TPU:25 now
where the time goes in v1:
time: 59.6 us; the launch traced here: 59.3 us
  Pallas kernels  54.9 us (92%)
  local copies, waits for them, and re-layouts  3.76 us (6%)
  between operations  0.66 us (1%)
    pallas_call x1, Pallas kernels, shards(): pl.pallas_call(functools.partial(kernel, ctx, hd, heads, count), out_shap...  54.9 us
    unnamed x7, local copies, waits for them, and re-layouts  3.76 us

profile of v1, /device:TPU:25, one launch (start us, length us, event | category | flops | bytes accessed | tf_op | source)
XLA Modules:
  0.0 59.3 jit_solution(3028024574464727644)
XLA Ops:
  0.6 54.9 %shard_map.85 = (bf16[512,1280]{1,0:T(8,128)(2,1)}, f32[128,128]{1,0:T(8,128)}, f32[128,128]{1,0:T(8,128)}) custom-call(bf16[512,1280]{1,0:T(8,128)(2,1)} %xs.1, bf16[512,128]{1,0:T(8,128)(2,1)} %bm.1, bf16[512,128]{1,0:T(8,128)(2,1)} %cm.1, f32[20,512]{1,0:T(8,128)} %ld.1, s32[1,512]{1,0:T(1,128)} %bitcast.1, bf16[512,1280]{1,0:T(8,128)(2,1)} %dy.1), custom_call_target="tpu_custom_call" | custom-call | tf_op jit(solution)/shard_map/pallas_call | solution.py:394
  55.5 0.0 copy-start.1
  55.6 0.0 copy-start
  55.6 2.5 %copy.12 = bf16[512,1280]{1,0:T(8,128)(2,1)} copy(bf16[512,1280]{1,0:T(8,128)(2,1)} %get-tuple-element.6) | data formatting | bytes 2621440
  58.1 0.0 copy-done.1
  58.1 0.6 %copy.13 = f32[128,128]{1,0:T(8,128)} copy(f32[128,128]{1,0:T(8,128)S(1)} %copy-done.1) | data formatting | bytes 131072
  58.7 0.0 copy-done
  58.7 0.6 %copy.14 = f32[128,128]{1,0:T(8,128)} copy(f32[128,128]{1,0:T(8,128)S(1)} %copy-done) | data formatting | bytes 131072
Async XLA Ops:
  55.5 2.5 %copy-start.1 = (f32[128,128]{1,0:T(8,128)S(1)}, f32[128,128]{1,0:T(8,128)}, u32[]{:S(2)}) copy-start(f32[128,128]{1,0:T(8,128)} %get-tuple-element.7) | copy-start | bytes 196612
  55.6 3.1 %copy-start = (f32[128,128]{1,0:T(8,128)S(1)}, f32[128,128]{1,0:T(8,128)}, u32[]{:S(2)}) copy-start(f32[128,128]{1,0:T(8,128)} %get-tuple-element.8) | copy-start | bytes 196612

commit v2 on v1

--- a/solution.py
+++ b/solution.py
@@ -11,6 +11,8 @@
 N = 128
 Q = 256
 LANES = 128
+WIDE = 256
+STRIDE = 32
 LOG2E = 1.4426950408889634
 MESH = pl.DeviceIdType.MESH
 F32 = jnp.float32
@@ -46,9 +48,9 @@
 
 def kernel(
     ctx, hd, heads, count,
-    xs, bm, cm, ld, st, dy,
+    xs_hbm, bm, cm, ld, st, dy_hbm,
     gx_out, gb_out, gc_out,
-    ldp, colterm, runrow, factor, expand, passing, bias, scores, mixed,
+    xs, dy, stacked, local_sem, ldp, colterm, runrow, factor, expand, passing, bias, scores, mixed,
     keys_t, reads_t, tail_x, t_hi, t_lo, e_hi, e_lo, group, local_s, local_a,
     agg, got0, chip, got, inout, other, final, part, rs_got,
     send_sem, recv_sem, rs_send, rs_recv,
@@ -62,6 +64,12 @@
     mate = [me + (1 - 2 * bit[d]) * (1 << d) for d in range(bits)]
     core = bit[0]
 
+    loads = [
+        pltpu.make_async_copy(xs_hbm, xs, local_sem.at[0]),
+        pltpu.make_async_copy(dy_hbm, dy, local_sem.at[1]),
+    ]
+    for copy in loads:
+        copy.start()
     barrier = pltpu.get_barrier_semaphore()
     for d in range(bits):
         pl.semaphore_signal(barrier, inc=1, device_id={"ctx": mate[d]}, device_id_type=MESH)
@@ -81,12 +89,21 @@
     tri = jnp.where(rows_i >= cols_i, 1.0, 0.0).astype(BF16)
     eye = jnp.where(rows_i == cols_i, 1.0, 0.0).astype(BF16)
     ldp[...] = jnp.zeros_like(ldp)
-    ldp[0:heads, :] = ld[...]
+    for i in range(3):
+        ldp[i * STRIDE : i * STRIDE + heads, :] = ld[...]
+    lane = lax.broadcasted_iota(jnp.int32, (1, LANES), 1)
     er = lax.broadcasted_iota(jnp.int32, (LANES, width), 0)
     ec = lax.broadcasted_iota(jnp.int32, (LANES, width), 1)
+    first = (er % STRIDE) * P_SIZE
     expand[...] = jnp.where(
-        (ec >= er * P_SIZE) & (ec < er * P_SIZE + P_SIZE), 1.0, 0.0
+        (ec >= first) & (ec < first + P_SIZE) & (er < 3 * STRIDE), 1.0, 0.0
     ).astype(BF16)
+
+    def packed(value):
+        high, middle, low = split3(value)
+        rest = jnp.where(lane < 2 * STRIDE, middle.astype(F32), low.astype(F32))
+        return jnp.where(lane < STRIDE, high.astype(F32), rest).astype(BF16)
+
     hp = runrow.shape[1]
     for b in range(count):
         blk = slice(b * Q, (b + 1) * Q)
@@ -105,12 +122,9 @@
         tail = jnp.where(seg_col == seg_last, jnp.exp(last - run), 0.0) * gain
         enter = jnp.where(seg_col == 0.0, jnp.exp(run), 0.0)
         through = jnp.broadcast_to(jnp.where(seg_last == 0.0, jnp.exp(last), 0.0), (16, LANES))
-        for i, value in enumerate(split3(tail)):
-            factor[b, 0, i] = value
-        for i, value in enumerate(split3(enter)):
-            factor[b, 1, i] = value
-        p3 = split3(through)
-        passing[b] = (nn(p3[0], expand[...]) + nn(p3[1], expand[...]) + nn(p3[2], expand[...]))[0:8]
+        factor[b, 0] = packed(tail)
+        factor[b, 1] = packed(enter)
+        passing[b] = nn(packed(through), expand[...])[0:8]
         keep = (cols_i >= rows_i) & (
             jnp.broadcast_to(seg_row[0:1], (Q, Q)) == jnp.broadcast_to(seg_col[:, 0:1], (Q, Q))
         )
@@ -119,38 +133,45 @@
         reads_t[b] = nt(eye[0:N, 0:N], cm[blk, :]).astype(BF16)
         scores[b] = nt(bm[blk, :], cm[blk, :])
 
-    for k in range(tiles):
-        col = slice(k * LANES, (k + 1) * LANES)
-        ex = expand[:, col]
+    pl.semaphore_wait(barrier, bits + hd - 1)
+    for copy in loads:
+        copy.wait()
+
+    def states(w):
+        wide = slice(w * WIDE, (w + 1) * WIDE)
+        ex = expand[:, wide]
         for b in range(count):
             blk = slice(b * Q, (b + 1) * Q)
-            tx = nn(factor[b, 0, 0], ex) + (nn(factor[b, 0, 1], ex) + nn(factor[b, 0, 2], ex))
-            tail_x[blk, col] = tx
-            hi, lo = split2(xs[blk, col].astype(F32) * tx)
-            t_hi[blk, col] = hi
-            t_lo[blk, col] = lo
-            local_s[b, k] = nn(keys_t[b], hi) + nn(keys_t[b], lo)
-            ent = nn(factor[b, 1, 0], ex) + (nn(factor[b, 1, 1], ex) + nn(factor[b, 1, 2], ex))
-            hi, lo = split2(dy[blk, col].astype(F32) * ent)
-            e_hi[blk, col] = hi
-            e_lo[blk, col] = lo
-            local_a[b, k] = nn(reads_t[b], hi) + nn(reads_t[b], lo)
-        forward, backward, through = local_s[0, k], local_a[count - 1, k], passing[0, :, col]
-        for b in range(1, count):
-            forward = local_s[b, k] + passing[b, 0:1, col] * forward
-            through = through * passing[b, :, col]
-        for b in range(count - 2, -1, -1):
-            backward = local_a[b, k] + passing[b, 0:1, col] * backward
-        agg[k, 0:N] = forward
-        agg[k, N : 2 * N] = backward
-        agg[k, 2 * N : 2 * N + 8] = through
-
-    pl.semaphore_wait(barrier, bits + hd - 1)
-    stage0 = [
-        remote(agg.at[(1 - core) * half + k], got0.at[k], 0, k, 0) for k in range(half)
-    ]
-    for copy in stage0:
-        copy.start()
+            tx = nn(factor[b, 0], ex)
+            tail_x[blk, wide] = tx
+            hi, lo = split2(xs[blk, wide].astype(F32) * tx)
+            t_hi[blk, wide] = hi
+            t_lo[blk, wide] = lo
+            own = nn(keys_t[b], hi) + nn(keys_t[b], lo)
+            local_s[b, 2 * w] = own[:, :LANES]
+            local_s[b, 2 * w + 1] = own[:, LANES:]
+            hi, lo = split2(dy[blk, wide].astype(F32) * nn(factor[b, 1], ex))
+            e_hi[blk, wide] = hi
+            e_lo[blk, wide] = lo
+            own = nn(reads_t[b], hi) + nn(reads_t[b], lo)
+            local_a[b, 2 * w] = own[:, :LANES]
+            local_a[b, 2 * w + 1] = own[:, LANES:]
+        for k in (2 * w, 2 * w + 1):
+            col = slice(k * LANES, (k + 1) * LANES)
+            forward, backward, through = local_s[0, k], local_a[count - 1, k], passing[0, :, col]
+            for b in range(1, count):
+                forward = local_s[b, k] + passing[b, 0:1, col] * forward
+                through = through * passing[b, :, col]
+            for b in range(count - 2, -1, -1):
+                backward = local_a[b, k] + passing[b, 0:1, col] * backward
+            agg[k, 0:N] = forward
+            agg[k, N : 2 * N] = backward
+            agg[k, 2 * N : 2 * N + 8] = through
+
+    def owned(core, k):
+        return core * half + (k + (half - 1) * (1 - core)) % half
+
+    stage0 = [remote(agg.at[owned(1 - core, k)], got0.at[k], 0, k, 0) for k in range(half)]
 
     F, B, T = slice(0, N), slice(N, 2 * N), slice(2 * N, 2 * N + 8)
     T1 = slice(2 * N, 2 * N + 1)
@@ -182,7 +203,7 @@
     def stage_core(k):
         stage0[k].wait_recv()
         merge(
-            chip.at[0, k], lambda s: agg[core * half + k, s], lambda s: got0[k, s], core == 1
+            chip.at[0, k], lambda s: agg[owned(core, k), s], lambda s: got0[k, s], core == 1
         )
         inout[k] = jnp.zeros((2 * N, LANES), F32)
         ahead[k] = (jnp.ones((1, LANES), F32), jnp.ones((1, LANES), F32))
@@ -205,7 +226,7 @@
             merge(chip.at[d, k], lambda s: mine[s], lambda s: theirs[s], upper)
             chip_send(d + 1, k)
         else:
-            own = agg.at[core * half + k]
+            own = agg.at[owned(core, k)]
             odd = core == 1
             enter0, leave1 = inout[k, F], inout[k, B]
             low_f = jnp.where(odd, got0[k, F], own[F])
@@ -214,16 +235,15 @@
             high_t = jnp.where(odd, own[T1], got0[k, T1])
             enter1 = low_f + low_t * enter0
             leave0 = high_b + high_t * leave1
-            final[core * half + k, F] = jnp.where(odd, enter1, enter0)
-            final[core * half + k, B] = jnp.where(odd, leave1, leave0)
+            final[owned(core, k), F] = jnp.where(odd, enter1, enter0)
+            final[owned(core, k), B] = jnp.where(odd, leave1, leave0)
             other[k, F] = jnp.where(odd, enter0, enter1)
             other[k, B] = jnp.where(odd, leave0, leave1)
-            copy = remote(other.at[k], final.at[core * half + k], bits, k, 0)
+            copy = remote(other.at[k], final.at[owned(core, k)], bits, k, 0)
             copies[bits, k] = copy
             copy.start()
 
     mixed[...] = jnp.zeros_like(mixed)
-    lane = lax.broadcasted_iota(jnp.int32, (1, LANES), 1)
     head_mask = [
         jnp.where(lane < P_SIZE, 1.0, 0.0).astype(BF16),
         jnp.where(lane < P_SIZE, 0.0, 1.0).astype(BF16),
@@ -255,16 +275,27 @@
                 mixed[b, s_in, t0:] += mix
                 group[s_at, col] = total
 
-    todo = {0: [("core", k) for k in range(half)]}
+    wides = width // WIDE
+    middle = wides // 2
+    states(middle)
+    stage0[0].start()
+    for w in range(middle):
+        states(w)
+        states(middle + 1 + w)
+        for k in (2 * w + 1, 2 * w + 2):
+            stage0[k].start()
+        for k in range(max(0, 2 * w - 1), 2 * w + 1):
+            stage_core(k)
+    intra(0)
+    for k in range(half - 2, half):
+        stage_core(k)
+    todo = {}
     for k in range(half):
-        todo.setdefault(min(2 * k + 2, tiles - 1), []).append(("chip", 1, k))
-    for k in range(tiles):
+        todo.setdefault(min(2 * k + 2, tiles - 1), []).append((1, k))
+    for k in range(1, tiles):
         intra(k)
-        for task in todo.get(k, []):
-            if task[0] == "core":
-                stage_core(task[1])
-            else:
-                stage_chip(task[1], task[2])
+        for d, at in todo.get(k, []):
+            stage_chip(d, at)
     for b in range(count):
         blk = slice(b * Q, (b + 1) * Q)
         hi, lo = split2(mixed[b])
@@ -286,31 +317,34 @@
             device_id={"head": dest}, device_id_type=MESH,
         )
 
-    def state_of(b, k, forward):
-        col = slice(k * LANES, (k + 1) * LANES)
-        if forward:
-            value = final[k, F]
-            for at in range(b):
-                value = local_s[at, k] + passing[at, 0:1, col] * value
-        else:
-            value = final[k, B]
-            for at in range(count - 1, b, -1):
-                value = local_a[at, k] + passing[at, 0:1, col] * value
-        return split2(value)
+    def state_of(b, w, forward):
+        wide = slice(w * WIDE, (w + 1) * WIDE)
+        rows, chain = (F, range(b)) if forward else (B, range(count - 1, b, -1))
+        local = local_s if forward else local_a
+        value = jnp.concatenate([final[2 * w, rows], final[2 * w + 1, rows]], axis=1)
+        for at in chain:
+            value = (
+                jnp.concatenate([local[at, 2 * w], local[at, 2 * w + 1]], axis=1)
+                + passing[at, 0:1, wide] * value
+            )
+        return jnp.concatenate(split2(value), axis=0)
 
     for b in range(count):
         blk = slice(b * Q, (b + 1) * Q)
-        key, read = part[0, blk], part[1, blk]
-        for k in range(tiles):
-            col = slice(k * LANES, (k + 1) * LANES)
-            hi, lo = state_of(b, k, False)
-            x_hi = t_hi[blk, col]
-            key += nt(x_hi, hi) + (nt(x_hi, lo) + nt(t_lo[blk, col], hi))
-            hi, lo = state_of(b, k, True)
-            y_hi = e_hi[blk, col]
-            read += nt(y_hi, hi) + (nt(y_hi, lo) + nt(e_lo[blk, col], hi))
-        part[0, blk] = key
-        part[1, blk] = read
+        key, read, key2, read2 = part[0, blk], part[1, blk], None, None
+        for w in range(wides):
+            wide = slice(w * WIDE, (w + 1) * WIDE)
+            both = state_of(b, w, False)
+            stacked[b, w] = both
+            product = nt(t_hi[blk, wide], both)
+            key2 = product if w == 0 else key2 + product
+            key += nt(t_lo[blk, wide], both[0:N])
+            both = state_of(b, w, True)
+            product = nt(e_hi[blk, wide], both)
+            read2 = product if w == 0 else read2 + product
+            read += nt(e_lo[blk, wide], both[0:N])
+        part[0, blk] = key + (key2[:, :N] + key2[:, N:])
+        part[1, blk] = read + (read2[:, :N] + read2[:, N:])
         for dest in range(hd):
             if b * Q < (dest + 1) * share <= (b + 1) * Q:
                 @pl.when(row != dest)
@@ -318,11 +352,11 @@
                     rs_copy(dest).start()
     for b in range(count):
         blk = slice(b * Q, (b + 1) * Q)
-        for k in range(tiles):
-            col = slice(k * LANES, (k + 1) * LANES)
-            hi, lo = state_of(b, k, False)
-            state_x = nn(bm[blk, :], hi) + nn(bm[blk, :], lo)
-            gx_out[blk, col] = (group[blk, col] + state_x * tail_x[blk, col]).astype(BF16)
+        keys2 = jnp.concatenate([bm[blk, :], bm[blk, :]], axis=1)
+        for w in range(wides):
+            wide = slice(w * WIDE, (w + 1) * WIDE)
+            state_x = nn(keys2, stacked[b, w])
+            gx_out[blk, wide] = (group[blk, wide] + state_x * tail_x[blk, wide]).astype(BF16)
     mine = pl.ds(pl.multiple_of(row * share, share), share)
     gb_out[...] = part[0, mine]
     gc_out[...] = part[1, mine]
@@ -357,10 +391,14 @@
     share = tokens // hd
     packet = 2 * N + 8
     scratch = [
+        pltpu.VMEM((tokens, width), BF16),
+        pltpu.VMEM((tokens, width), BF16),
+        pltpu.VMEM((count, width // WIDE, 2 * N, WIDE), BF16),
+        pltpu.SemaphoreType.DMA((2 + count,)),
         pltpu.VMEM((LANES, tokens), F32),
         pltpu.VMEM((count, Q, LANES), F32),
         pltpu.VMEM((count, head_rows, Q), F32),
-        pltpu.VMEM((count, 2, 3, Q, LANES), BF16),
+        pltpu.VMEM((count, 2, Q, LANES), BF16),
         pltpu.VMEM((LANES, width), BF16),
         pltpu.VMEM((count, 8, width), F32),
         pltpu.VMEM((count, Q, Q), F32),
@@ -391,20 +429,22 @@
         pltpu.SemaphoreType.DMA((hd,)),
     ]
     vmem = pl.BlockSpec(memory_space=pltpu.VMEM)
-    return pl.pallas_call(
+    anywhere = pl.BlockSpec(memory_space=pl.ANY)
+    results = pl.pallas_call(
         functools.partial(kernel, ctx, hd, heads, count),
         out_shape=(
-            jax.ShapeDtypeStruct((tokens, width), BF16),
-            jax.ShapeDtypeStruct((share, N), F32),
-            jax.ShapeDtypeStruct((share, N), F32),
+            pltpu.VMEM((tokens, width), BF16),
+            pltpu.VMEM((share, N), F32),
+            pltpu.VMEM((share, N), F32),
         ),
-        in_specs=[vmem] * 6,
-        out_specs=(vmem,) * 3,
+        in_specs=[anywhere, vmem, vmem, vmem, vmem, anywhere],
+        out_specs=(vmem, vmem, vmem),
         scratch_shapes=scratch,
         compiler_params=pltpu.CompilerParams(
             collective_id=0, has_side_effects=True, vmem_limit_bytes=56 * 1024 * 1024
         ),
     )(xs, bmat, cmat, logdecay, starts.reshape(1, tokens), output_cotangent)
+    return results
 
 
 def solution(mesh):

time: 59.6 us -> 44.7 us (0.75)
  Pallas kernels: 54.9 us -> 41.6 us
  local copies, waits for them, and re-layouts: 3.76 us -> 2.32 us
    pallas_call x1, Pallas kernels: 54.9 us -> 41.6 us  [shards(): pl.pallas_call(functools.partial(kernel, ctx, hd, heads, count), out_shap...]
    unnamed x7 -> x3, local copies, waits for them, and re-layouts: 3.76 us -> 2.32 us
where the time goes in v2:
time: 44.7 us; the launch traced here: 44.6 us
  Pallas kernels  41.6 us (93%)
  local copies, waits for them, and re-layouts  2.32 us (5%)
  between operations  0.64 us (1%)
    pallas_call x1, Pallas kernels, shards(): pl.pallas_call(functools.partial(kernel, ctx, hd, heads, count), out_shap...  41.6 us
    unnamed x3, local copies, waits for them, and re-layouts  2.32 us

profile of v2, /device:TPU:25, one launch (start us, length us, event | category | flops | bytes accessed | tf_op | source)
XLA Modules:
  0.0 44.6 jit_solution(11717221100217761012)
XLA Ops:
  0.6 41.6 %shard_map.85 = (bf16[512,1280]{1,0:T(8,128)(2,1)S(1)}, f32[128,128]{1,0:T(8,128)S(1)}, f32[128,128]{1,0:T(8,128)S(1)}) custom-call(bf16[512,1280]{1,0:T(8,128)(2,1)} %xs_hbm.1, bf16[512,128]{1,0:T(8,128)(2,1)} %bm.1, bf16[512,128]{1,0:T(8,128)(2,1)} %cm.1, f32[20,512]{1,0:T(8,128)} %ld.1, s32[1,512]{1,0:T(1,128)} %bitcast.1, bf16[512,1280]{1,0:T(8,128)(2,1)} %dy_hbm.1), custom_call_target="tpu_custom_call" | custom-call | tf_op jit(solution)/shard_map/pallas_call | solution.py:433
  42.2 1.1 %copy.12 = bf16[512,1280]{1,0:T(8,128)(2,1)} copy(bf16[512,1280]{1,0:T(8,128)(2,1)S(1)} %get-tuple-element.3) | data formatting | bytes 2621440
  43.3 0.6 %copy.13 = f32[128,128]{1,0:T(8,128)} copy(f32[128,128]{1,0:T(8,128)S(1)} %get-tuple-element.4) | data formatting | bytes 131072
  43.9 0.6 %copy.14 = f32[128,128]{1,0:T(8,128)} copy(f32[128,128]{1,0:T(8,128)S(1)} %get-tuple-element.5) | data formatting | bytes 131072

commit v3 on v2

--- a/solution.py
+++ b/solution.py
@@ -50,7 +50,7 @@
     ctx, hd, heads, count,
     xs_hbm, bm, cm, ld, st, dy_hbm,
     gx_out, gb_out, gc_out,
-    xs, dy, stacked, local_sem, ldp, colterm, runrow, factor, expand, passing, bias, scores, mixed,
+    xs, dy, stacked, local_sem, more, pair, across, ldp, colterm, runrow, factor, expand, passing, bias, scores, mixed,
     keys_t, reads_t, tail_x, t_hi, t_lo, e_hi, e_lo, group, local_s, local_a,
     agg, got0, chip, got, inout, other, final, part, rs_got,
     send_sem, recv_sem, rs_send, rs_recv,
@@ -136,6 +136,10 @@
     pl.semaphore_wait(barrier, bits + hd - 1)
     for copy in loads:
         copy.wait()
+
+    F, T, T1 = slice(0, N), slice(N, N + 8), slice(N, N + 1)
+    B, TB = slice(N + 8, 2 * N + 8), slice(2 * N + 8, 2 * N + 16)
+    portion = N + 8
 
     def states(w):
         wide = slice(w * WIDE, (w + 1) * WIDE)
@@ -164,17 +168,18 @@
                 through = through * passing[b, :, col]
             for b in range(count - 2, -1, -1):
                 backward = local_a[b, k] + passing[b, 0:1, col] * backward
-            agg[k, 0:N] = forward
-            agg[k, N : 2 * N] = backward
-            agg[k, 2 * N : 2 * N + 8] = through
+            agg[k, F] = forward
+            agg[k, T] = through
+            agg[k, B] = backward
+            agg[k, TB] = through
 
     def owned(core, k):
         return core * half + (k + (half - 1) * (1 - core)) % half
 
     stage0 = [remote(agg.at[owned(1 - core, k)], got0.at[k], 0, k, 0) for k in range(half)]
 
-    F, B, T = slice(0, N), slice(N, 2 * N), slice(2 * N, 2 * N + 8)
-    T1 = slice(2 * N, 2 * N + 1)
+    I, O = slice(0, N), slice(N, 2 * N)
+    forwarded = 2
     copies = {}
     ahead = {}
 
@@ -187,18 +192,41 @@
 
         target[F] = high(F) + high(T1) * low(F)
         target[B] = low(B) + low(T1) * high(B)
-        target[T] = low(T) * high(T)
+        through = low(T) * high(T)
+        target[T] = through
+        target[TB] = through
+
+    near, far = bits - 2, bits - 1
+    lo_bit, hi_bit = bit[near], bit[far]
+    inner = lo_bit + hi_bit == 1
+    outer = lo_bit + hi_bit != 1
+    started = []
+
+    def begin(copy, condition=None):
+        started.append((copy, condition))
+        guarded(copy.start, condition)
+        return copy
+
+    def guarded(action, condition):
+        if condition is None:
+            action()
+        else:
+            pl.when(condition)(action)
 
     def chip_send(d, k):
-        if d == bits - 1:
-            copy = remote(
-                chip.at[d - 1, k, pl.ds(pl.multiple_of(bit[d] * N, N), N)],
-                got.at[d - 1, k, pl.ds(0, N)], d, k, d,
-            )
-        else:
-            copy = remote(chip.at[d - 1, k], got.at[d - 1, k], d, k, d)
-        copies[d, k] = copy
-        copy.start()
+        if d < near:
+            copies[d, k] = begin(remote(chip.at[d - 1, k], got.at[d - 1, k], d, k, d))
+            return
+        source = chip.at[d - 1, k]
+        copies["near", k] = begin(remote(
+            source.at[pl.ds(pl.multiple_of(lo_bit * portion, 8), portion)],
+            got.at[d - 1, k, pl.ds(0, portion)], near, k, near,
+        ))
+        if k >= forwarded:
+            copies["more", k] = begin(remote(
+                source.at[pl.ds(pl.multiple_of((1 - lo_bit) * portion, 8), N)],
+                more.at[k], bits + 1, k, near,
+            ), inner)
 
     def stage_core(k):
         stage0[k].wait_recv()
@@ -213,35 +241,58 @@
         copies[d, k].wait_recv()
         upper = bit[d] == 1
         from_before, from_after = ahead[k]
-        theirs = got.at[d - 1, k]
-        last = d == bits - 1
-        inout[k, F] = inout[k, F] + jnp.where(upper, from_before, 0.0) * theirs[F]
-        inout[k, B] = inout[k, B] + jnp.where(upper, 0.0, from_after) * theirs[F if last else B]
-        if not last:
-            ahead[k] = (
-                jnp.where(upper, from_before * theirs[T1], from_before),
-                jnp.where(upper, from_after, from_after * theirs[T1]),
-            )
-            mine = chip.at[d - 1, k]
-            merge(chip.at[d, k], lambda s: mine[s], lambda s: theirs[s], upper)
-            chip_send(d + 1, k)
+        theirs, mine = got.at[d - 1, k], chip.at[d - 1, k]
+        inout[k, I] = inout[k, I] + jnp.where(upper, from_before, 0.0) * theirs[F]
+        inout[k, O] = inout[k, O] + jnp.where(upper, 0.0, from_after) * theirs[B]
+        ahead[k] = (
+            jnp.where(upper, from_before * theirs[T1], from_before),
+            jnp.where(upper, from_after, from_after * theirs[T1]),
+        )
+        merge(chip.at[d, k], lambda s: mine[s], lambda s: theirs[s], upper)
+        chip_send(d + 1, k)
+
+    def stage_near(k):
+        copies["near", k].wait_recv()
+        theirs, mine = got.at[near - 1, k], chip.at[near - 1, k]
+        own = jnp.where(hi_bit == 0, mine[F], mine[B])
+        both = own + mine[T1] * theirs[F]
+        if k >= forwarded:
+            guarded(copies["more", k].wait_recv, outer)
+            both = jnp.where(inner, both, more[k] + theirs[T1] * own)
+        pair[k] = both
+        copies["far", k] = begin(
+            remote(pair.at[k], across.at[k], far, k, far), inner if k < forwarded else None
+        )
+
+    def stage_forward(k):
+        guarded(copies["far", k].wait_recv, outer)
+        copies["on", k] = begin(remote(across.at[k], across.at[k], bits + 2, k, near), outer)
+
+    def stage_far(k):
+        if k < forwarded:
+            guarded(copies["on", k].wait_recv, inner)
         else:
-            own = agg.at[owned(core, k)]
-            odd = core == 1
-            enter0, leave1 = inout[k, F], inout[k, B]
-            low_f = jnp.where(odd, got0[k, F], own[F])
-            low_t = jnp.where(odd, got0[k, T1], own[T1])
-            high_b = jnp.where(odd, own[B], got0[k, B])
-            high_t = jnp.where(odd, own[T1], got0[k, T1])
-            enter1 = low_f + low_t * enter0
-            leave0 = high_b + high_t * leave1
-            final[owned(core, k), F] = jnp.where(odd, enter1, enter0)
-            final[owned(core, k), B] = jnp.where(odd, leave1, leave0)
-            other[k, F] = jnp.where(odd, enter0, enter1)
-            other[k, B] = jnp.where(odd, leave0, leave1)
-            copy = remote(other.at[k], final.at[owned(core, k)], bits, k, 0)
-            copies[bits, k] = copy
-            copy.start()
+            copies["far", k].wait_recv()
+        theirs, beyond = got.at[near - 1, k], across[k]
+        near_side = jnp.where(inner, theirs[F], theirs[F] + theirs[T1] * beyond)
+        from_before, from_after = ahead[k]
+        far_before = jnp.where(hi_bit == 1, beyond, 0.0)
+        far_after = jnp.where(hi_bit == 0, beyond, 0.0)
+        enter0 = inout[k, I] + from_before * jnp.where(lo_bit == 1, near_side, far_before)
+        leave1 = inout[k, O] + from_after * jnp.where(lo_bit == 0, near_side, far_after)
+        own = agg.at[owned(core, k)]
+        odd = core == 1
+        low_f = jnp.where(odd, got0[k, F], own[F])
+        low_t = jnp.where(odd, got0[k, T1], own[T1])
+        high_b = jnp.where(odd, own[B], got0[k, B])
+        high_t = jnp.where(odd, own[T1], got0[k, T1])
+        enter1 = low_f + low_t * enter0
+        leave0 = high_b + high_t * leave1
+        final[owned(core, k), I] = jnp.where(odd, enter1, enter0)
+        final[owned(core, k), O] = jnp.where(odd, leave1, leave0)
+        other[k, I] = jnp.where(odd, enter0, enter1)
+        other[k, O] = jnp.where(odd, leave0, leave1)
+        copies["core", k] = begin(remote(other.at[k], final.at[owned(core, k)], bits, k, 0))
 
     mixed[...] = jnp.zeros_like(mixed)
     head_mask = [
@@ -289,24 +340,33 @@
     intra(0)
     for k in range(half - 2, half):
         stage_core(k)
-    todo = {}
-    for k in range(half):
-        todo.setdefault(min(2 * k + 2, tiles - 1), []).append((1, k))
     for k in range(1, tiles):
         intra(k)
-        for d, at in todo.get(k, []):
-            stage_chip(d, at)
+        if near == 1 and k in (4, 7):
+            stage_near(0 if k == 4 else 1)
     for b in range(count):
         blk = slice(b * Q, (b + 1) * Q)
         hi, lo = split2(mixed[b])
         part[0, blk] = nn(hi, cm[blk, :]) + nn(lo, cm[blk, :])
         hi, lo = split2(mixed[b].T)
         part[1, blk] = nn(hi, bm[blk, :]) + nn(lo, bm[blk, :])
-    for d in range(2, bits):
+    for d in range(1, near):
         for k in range(half):
             stage_chip(d, k)
+    if near > 1:
+        for k in range(forwarded):
+            stage_near(k)
+    for k in range(forwarded):
+        stage_forward(k)
+    stage_near(2)
+    for k in range(forwarded):
+        stage_far(k)
+    for k in range(3, half):
+        stage_near(k)
+        stage_far(k - 1)
+    stage_far(half - 1)
     for k in range(half):
-        copies[bits, k].wait_recv()
+        copies["core", k].wait_recv()
 
     share = count * Q // hd
 
@@ -319,7 +379,7 @@
 
     def state_of(b, w, forward):
         wide = slice(w * WIDE, (w + 1) * WIDE)
-        rows, chain = (F, range(b)) if forward else (B, range(count - 1, b, -1))
+        rows, chain = (I, range(b)) if forward else (O, range(count - 1, b, -1))
         local = local_s if forward else local_a
         value = jnp.concatenate([final[2 * w, rows], final[2 * w + 1, rows]], axis=1)
         for at in chain:
@@ -376,8 +436,8 @@
             rs_copy(dest).wait_send()
     for copy in stage0:
         copy.wait_send()
-    for copy in copies.values():
-        copy.wait_send()
+    for copy, condition in started:
+        guarded(copy.wait_send, condition)
 
 
 def shards(ctx, hd, xs, bmat, cmat, logdecay, starts, output_cotangent):
@@ -389,12 +449,15 @@
     bits = ctx.bit_length() - 1
     head_rows = (heads + 15) // 16 * 16
     share = tokens // hd
-    packet = 2 * N + 8
+    packet = 2 * N + 16
     scratch = [
         pltpu.VMEM((tokens, width), BF16),
         pltpu.VMEM((tokens, width), BF16),
         pltpu.VMEM((count, width // WIDE, 2 * N, WIDE), BF16),
-        pltpu.SemaphoreType.DMA((2 + count,)),
+        pltpu.SemaphoreType.DMA((2,)),
+        pltpu.VMEM((half, N, LANES), F32),
+        pltpu.VMEM((half, N, LANES), F32),
+        pltpu.VMEM((half, N, LANES), F32),
         pltpu.VMEM((LANES, tokens), F32),
         pltpu.VMEM((count, Q, LANES), F32),
         pltpu.VMEM((count, head_rows, Q), F32),
@@ -423,8 +486,8 @@
         pltpu.VMEM((tiles, 2 * N, LANES), F32),
         pltpu.VMEM((2, tokens, N), F32),
         pltpu.VMEM((hd, 2, share, N), F32),
-        pltpu.SemaphoreType.DMA((bits + 1, half)),
-        pltpu.SemaphoreType.DMA((bits + 1, half)),
+        pltpu.SemaphoreType.DMA((bits + 3, half)),
+        pltpu.SemaphoreType.DMA((bits + 3, half)),
         pltpu.SemaphoreType.DMA((hd,)),
         pltpu.SemaphoreType.DMA((hd,)),
     ]

time: 44.7 us -> 42.3 us (0.946)
  Pallas kernels: 41.6 us -> 39.1 us
    pallas_call x1, Pallas kernels: 41.6 us -> 39.1 us  [shards(): pl.pallas_call(functools.partial(kernel, ctx, hd, heads, count), out_shap...]
where the time goes in v3:
time: 42.3 us; the launch traced here: 42.1 us
  Pallas kernels  39.1 us (92%)
  local copies, waits for them, and re-layouts  2.32 us (5%)
  between operations  0.64 us (2%)
    pallas_call x1, Pallas kernels, shards(): pl.pallas_call(functools.partial(kernel, ctx, hd, heads, count), out_shap...  39.1 us
    unnamed x3, local copies, waits for them, and re-layouts  2.32 us

profile of v3, /device:TPU:25, one launch (start us, length us, event | category | flops | bytes accessed | tf_op | source)
XLA Modules:
  0.0 42.1 jit_solution(3213094333961582187)
XLA Ops:
  0.6 39.1 %shard_map.85 = (bf16[512,1280]{1,0:T(8,128)(2,1)S(1)}, f32[128,128]{1,0:T(8,128)S(1)}, f32[128,128]{1,0:T(8,128)S(1)}) custom-call(bf16[512,1280]{1,0:T(8,128)(2,1)} %xs_hbm.1, bf16[512,128]{1,0:T(8,128)(2,1)} %bm.1, bf16[512,128]{1,0:T(8,128)(2,1)} %cm.1, f32[20,512]{1,0:T(8,128)} %ld.1, s32[1,512]{1,0:T(1,128)} %bitcast.1, bf16[512,1280]{1,0:T(8,128)(2,1)} %dy_hbm.1), custom_call_target="tpu_custom_call" | custom-call | tf_op jit(solution)/shard_map/pallas_call | solution.py:496
  39.8 1.1 %copy.12 = bf16[512,1280]{1,0:T(8,128)(2,1)} copy(bf16[512,1280]{1,0:T(8,128)(2,1)S(1)} %get-tuple-element.3) | data formatting | bytes 2621440
  40.8 0.6 %copy.13 = f32[128,128]{1,0:T(8,128)} copy(f32[128,128]{1,0:T(8,128)S(1)} %get-tuple-element.4) | data formatting | bytes 131072
  41.5 0.6 %copy.14 = f32[128,128]{1,0:T(8,128)} copy(f32[128,128]{1,0:T(8,128)S(1)} %get-tuple-element.5) | data formatting | bytes 131072

commit v4 on v3

--- a/solution.py
+++ b/solution.py
@@ -50,7 +50,7 @@
     ctx, hd, heads, count,
     xs_hbm, bm, cm, ld, st, dy_hbm,
     gx_out, gb_out, gc_out,
-    xs, dy, stacked, local_sem, more, pair, across, ldp, colterm, runrow, factor, expand, passing, bias, scores, mixed,
+    xs, dy, stacked, local_sem, more, pair, across, sums, ldp, colterm, runrow, factor, expand, passing, bias, scores, mixed,
     keys_t, reads_t, tail_x, t_hi, t_lo, e_hi, e_lo, group, local_s, local_a,
     agg, got0, chip, got, inout, other, final, part, rs_got,
     send_sem, recv_sem, rs_send, rs_recv,
@@ -356,19 +356,8 @@
     if near > 1:
         for k in range(forwarded):
             stage_near(k)
-    for k in range(forwarded):
-        stage_forward(k)
-    stage_near(2)
-    for k in range(forwarded):
-        stage_far(k)
-    for k in range(3, half):
-        stage_near(k)
-        stage_far(k - 1)
-    stage_far(half - 1)
-    for k in range(half):
-        copies["core", k].wait_recv()
-
     share = count * Q // hd
+    sums[...] = jnp.zeros_like(sums)
 
     def rs_copy(dest):
         return pltpu.make_async_remote_copy(
@@ -389,34 +378,59 @@
             )
         return jnp.concatenate(split2(value), axis=0)
 
+    def outside(b, w):
+        blk, wide = slice(b * Q, (b + 1) * Q), slice(w * WIDE, (w + 1) * WIDE)
+        both = state_of(b, w, False)
+        stacked[b, w] = both
+        sums[b, 0] += nt(t_hi[blk, wide], both)
+        part[0, blk] += nt(t_lo[blk, wide], both[0:N])
+        both = state_of(b, w, True)
+        sums[b, 1] += nt(e_hi[blk, wide], both)
+        part[1, blk] += nt(e_lo[blk, wide], both[0:N])
+
+    def gradient(b, w):
+        blk, wide = slice(b * Q, (b + 1) * Q), slice(w * WIDE, (w + 1) * WIDE)
+        keys2 = jnp.concatenate([bm[blk, :], bm[blk, :]], axis=1)
+        state_x = nn(keys2, stacked[b, w])
+        gx_out[blk, wide] = (group[blk, wide] + state_x * tail_x[blk, wide]).astype(BF16)
+
+    def finish(w):
+        for b in range(count):
+            outside(b, w)
+            gradient(b, w)
+
+    for k in range(forwarded):
+        stage_forward(k)
+    stage_near(2)
+    for k in range(forwarded):
+        stage_far(k)
+    stage_near(3)
+    stage_far(2)
+    copies["core", 0].wait_recv()
+    finish(wides // 2)
+    stage_near(4)
+    stage_far(3)
+    for k in (1, 2):
+        copies["core", k].wait_recv()
+    finish(0)
+    finish(wides // 2 + 1)
+    stage_far(4)
+    for k in (3, 4):
+        copies["core", k].wait_recv()
     for b in range(count):
         blk = slice(b * Q, (b + 1) * Q)
-        key, read, key2, read2 = part[0, blk], part[1, blk], None, None
-        for w in range(wides):
-            wide = slice(w * WIDE, (w + 1) * WIDE)
-            both = state_of(b, w, False)
-            stacked[b, w] = both
-            product = nt(t_hi[blk, wide], both)
-            key2 = product if w == 0 else key2 + product
-            key += nt(t_lo[blk, wide], both[0:N])
-            both = state_of(b, w, True)
-            product = nt(e_hi[blk, wide], both)
-            read2 = product if w == 0 else read2 + product
-            read += nt(e_lo[blk, wide], both[0:N])
-        part[0, blk] = key + (key2[:, :N] + key2[:, N:])
-        part[1, blk] = read + (read2[:, :N] + read2[:, N:])
+        outside(b, 1)
+        outside(b, wides - 1)
+        part[0, blk] += sums[b, 0, :, :N] + sums[b, 0, :, N:]
+        part[1, blk] += sums[b, 1, :, :N] + sums[b, 1, :, N:]
         for dest in range(hd):
             if b * Q < (dest + 1) * share <= (b + 1) * Q:
                 @pl.when(row != dest)
                 def _(dest=dest):
                     rs_copy(dest).start()
     for b in range(count):
-        blk = slice(b * Q, (b + 1) * Q)
-        keys2 = jnp.concatenate([bm[blk, :], bm[blk, :]], axis=1)
-        for w in range(wides):
-            wide = slice(w * WIDE, (w + 1) * WIDE)
-            state_x = nn(keys2, stacked[b, w])
-            gx_out[blk, wide] = (group[blk, wide] + state_x * tail_x[blk, wide]).astype(BF16)
+        for w in (1, wides - 1):
+            gradient(b, w)
     mine = pl.ds(pl.multiple_of(row * share, share), share)
     gb_out[...] = part[0, mine]
     gc_out[...] = part[1, mine]
@@ -458,6 +472,7 @@
         pltpu.VMEM((half, N, LANES), F32),
         pltpu.VMEM((half, N, LANES), F32),
         pltpu.VMEM((half, N, LANES), F32),
+        pltpu.VMEM((count, 2, Q, WIDE), F32),
         pltpu.VMEM((LANES, tokens), F32),
         pltpu.VMEM((count, Q, LANES), F32),
         pltpu.VMEM((count, head_rows, Q), F32),

time: 42.3 us -> 41.5 us (0.981)
  Pallas kernels: 39.1 us -> 38.4 us
    pallas_call x1, Pallas kernels: 39.1 us -> 38.4 us  [shards(): pl.pallas_call(functools.partial(kernel, ctx, hd, heads, count), out_shap...]
where the time goes in v4:
time: 41.5 us; the launch traced here: 41.4 us
  Pallas kernels  38.4 us (93%)
  local copies, waits for them, and re-layouts  2.32 us (6%)
  between operations  0.64 us (2%)
    pallas_call x1, Pallas kernels, shards(): pl.pallas_call(functools.partial(kernel, ctx, hd, heads, count), out_shap...  38.4 us
    unnamed x3, local copies, waits for them, and re-layouts  2.32 us

profile of v4, /device:TPU:25, one launch (start us, length us, event | category | flops | bytes accessed | tf_op | source)
XLA Modules:
  0.0 41.4 jit_solution(12667847946783196161)
XLA Ops:
  0.6 38.4 %shard_map.85 = (bf16[512,1280]{1,0:T(8,128)(2,1)S(1)}, f32[128,128]{1,0:T(8,128)S(1)}, f32[128,128]{1,0:T(8,128)S(1)}) custom-call(bf16[512,1280]{1,0:T(8,128)(2,1)} %xs_hbm.1, bf16[512,128]{1,0:T(8,128)(2,1)} %bm.1, bf16[512,128]{1,0:T(8,128)(2,1)} %cm.1, f32[20,512]{1,0:T(8,128)} %ld.1, s32[1,512]{1,0:T(1,128)} %bitcast.1, bf16[512,1280]{1,0:T(8,128)(2,1)} %dy_hbm.1), custom_call_target="tpu_custom_call" | custom-call | tf_op jit(solution)/shard_map/pallas_call | solution.py:511
  39.0 1.1 %copy.12 = bf16[512,1280]{1,0:T(8,128)(2,1)} copy(bf16[512,1280]{1,0:T(8,128)(2,1)S(1)} %get-tuple-element.3) | data formatting | bytes 2621440
  40.1 0.6 %copy.13 = f32[128,128]{1,0:T(8,128)} copy(f32[128,128]{1,0:T(8,128)S(1)} %get-tuple-element.4) | data formatting | bytes 131072
  40.7 0.6 %copy.14 = f32[128,128]{1,0:T(8,128)} copy(f32[128,128]{1,0:T(8,128)S(1)} %get-tuple-element.5) | data formatting | bytes 131072
